TPU v7x, 256 devices: a whole 4x4x8 slice. The times are simulated.
256 devices in a mesh: dp: 16 (over z, x_lo), frame: 16 (over x_hi, y, core).
Axes of the slice: x: 4 (x_hi: 2, x_lo: 2; x = x_hi * 2 + x_lo), y: 4, z: 8, core: 2. Of those that a mesh axis runs over, the one named last changes fastest.
Arguments:
- latents: bfloat16 [16, 16, 8, 16, 1280], P('dp', 'frame'), may hold values from -6 to 6
- out_grad: bfloat16 [16, 16, 8, 16, 1280], P('dp', 'frame'), may hold values from -6 to 6
- video: bfloat16 [16, 16, 16, 32, 1280], P('dp', 'frame'), may hold values from -6 to 6
- owner: int32 [16], P('dp'), may hold values from 0 to 15
- w_query: bfloat16 [1280, 640], replicated, may hold values from -0.15625 to 0.15625
- w_key: bfloat16 [1280, 640], replicated, may hold values from -0.15625 to 0.15625
- w_value: bfloat16 [1280, 640], replicated, may hold values from -0.15625 to 0.15625
- w_out: bfloat16 [640, 1280], replicated, may hold values from -0.25 to 0.25
Outputs:
- block_out: bfloat16 [16, 16, 8, 16, 1280], P('dp', 'frame')
- grad_latents: bfloat16 [16, 16, 8, 16, 1280], P('dp', 'frame')
- grad_weights: float32 [1280, 1280], P(('dp', 'frame'))
Inputs may be any that keep to these rules, and one draw needn't show every extreme that they name: owner[o] is the frame index of the device whose video slot holds object o's input video.
All inputs are finite; a program needn't handle non-finite values.
Results may differ from a plain program's by a relative error of at most 0.013.
Values may be sent and summed in bfloat16 or wider, within the bound.
A program may use at most 128 MiB of HBM per device.

v0:
```python
import jax
import jax.numpy as jnp
from jax import lax
from jax.sharding import PartitionSpec as P

HEADS = 10
HD = 64


def broadcast(value, axis, source):
    kept = jnp.where(lax.axis_index(axis) == source, value, 0).astype(value.dtype)
    return lax.psum(kept, axis)


def normalize(tensor):
    factor = lax.rsqrt(jnp.mean(tensor * tensor, axis=-1, keepdims=True) + 1e-06)
    return (tensor * factor, factor)


def to_half(tensor):
    return lax.optimization_barrier(tensor.astype(jnp.bfloat16)).astype(jnp.float32)


def frame_local(piece):
    scale_qk = HD ** (-0.5)
    span = piece.shape[0]
    count = piece.shape[1]
    inner = piece.shape[2] // 4
    shaped = (span, count, HEADS, HD)
    query = piece[:, :, :inner].reshape(shaped)
    key = piece[:, :, inner : 2 * inner].reshape(shaped)
    value = piece[:, :, 2 * inner : 3 * inner].reshape(shaped)
    grad_o = piece[:, :, 3 * inner :].reshape(shaped)
    query_f = query.astype(jnp.float32)
    grad_f = grad_o.astype(jnp.float32)
    tscore = (
        jnp.einsum("fnhd,gnhd->nhfg", query, key, preferred_element_type=jnp.float32) * scale_qk
    )
    texpo = jnp.exp(tscore)
    ttotal = jnp.sum(texpo, axis=-1)
    time_out = (
        jnp.einsum(
            "nhfg,gnhd->fnhd", texpo.astype(jnp.bfloat16), value, preferred_element_type=jnp.float32
        )
        / jnp.transpose(ttotal, (2, 0, 1))[..., None]
    )
    tprob = texpo / ttotal[..., None]
    dtprob = jnp.einsum("fnhd,gnhd->nhfg", grad_o, value, preferred_element_type=jnp.float32)
    tdelta = jnp.transpose(jnp.sum(grad_f * time_out, axis=-1), (1, 2, 0))
    dts = tprob * (dtprob - tdelta[..., None])
    dq_time = jnp.einsum("nhfg,gnhd->fnhd", dts, key.astype(jnp.float32)) * scale_qk
    dk_time = jnp.sum(to_half(jnp.einsum("nhfg,fnhd->fgnhd", dts, query_f) * scale_qk), axis=0)
    dv_time = jnp.sum(to_half(jnp.einsum("nhfg,fnhd->fgnhd", tprob, grad_f)), axis=0)
    flat = (span, count, inner)
    return jnp.concatenate(
        [
            time_out.reshape(flat),
            dq_time.reshape(flat),
            dk_time.reshape(flat),
            dv_time.reshape(flat),
        ],
        axis=-1,
    )


def shards(latents, out_grad, video, owner, w_query, w_key, w_value, w_out):
    inv = HD ** (-0.5)
    frames = lax.axis_size("frame")
    here = lax.axis_index("frame")
    rows = latents.shape[2] * latents.shape[3]
    width = latents.shape[4]
    inner = w_query.shape[1]
    xf = latents.reshape(rows, width).astype(jnp.float32)
    normed, factor = normalize(xf)
    xn = normed.astype(jnp.bfloat16)
    slab = broadcast(video[0, 0], "frame", owner[0])
    cond = lax.dynamic_index_in_dim(slab, here, 0, keepdims=False)
    cn = normalize(cond.astype(jnp.float32))[0].astype(jnp.bfloat16)
    vt_rows = cn.shape[0]
    query = jnp.dot(xn, w_query, preferred_element_type=jnp.float32).astype(jnp.bfloat16)
    key = jnp.dot(xn, w_key, preferred_element_type=jnp.float32).astype(jnp.bfloat16)
    value = jnp.dot(xn, w_value, preferred_element_type=jnp.float32).astype(jnp.bfloat16)
    key_c = jnp.dot(cn, w_key, preferred_element_type=jnp.float32).astype(jnp.bfloat16)
    value_c = jnp.dot(cn, w_value, preferred_element_type=jnp.float32).astype(jnp.bfloat16)
    grad_y = out_grad.reshape(rows, width)
    go = jnp.dot(grad_y, w_out.T, preferred_element_type=jnp.float32).astype(jnp.bfloat16)
    go3 = go.reshape(rows, HEADS, HD)
    gof = go3.astype(jnp.float32)
    q3 = query.reshape(rows, HEADS, HD)
    keys = jnp.concatenate([key, key_c], axis=0).reshape(rows + vt_rows, HEADS, HD)
    vals = jnp.concatenate([value, value_c], axis=0).reshape(rows + vt_rows, HEADS, HD)
    score = jnp.einsum("rhd,khd->hrk", q3, keys, preferred_element_type=jnp.float32) * inv
    expo = jnp.exp(score)
    tot = jnp.sum(expo, axis=-1)
    view_out = (
        jnp.einsum(
            "hrk,khd->rhd", expo.astype(jnp.bfloat16), vals, preferred_element_type=jnp.float32
        )
        / jnp.transpose(tot)[..., None]
    )
    group = rows // frames
    packed = jnp.concatenate([query, key, value, go], axis=1).reshape(frames, group, 4 * inner)
    local_out = frame_local(
        lax.all_to_all(packed, "frame", split_axis=0, concat_axis=0, tiled=True)
    )
    returned_all = (
        lax.all_to_all(
            local_out.astype(jnp.bfloat16), "frame", split_axis=0, concat_axis=0, tiled=True
        )
        .astype(local_out.dtype)
        .reshape(rows, 4 * inner)
    )
    time_out = returned_all[:, :inner].reshape(rows, HEADS, HD)
    dq_time = returned_all[:, inner : 2 * inner].reshape(rows, HEADS, HD)
    dk_time = returned_all[:, 2 * inner : 3 * inner]
    dv_time = returned_all[:, 3 * inner :]
    hidden = (view_out + time_out).reshape(rows, inner).astype(jnp.bfloat16)
    block = (xf + jnp.dot(hidden, w_out, preferred_element_type=jnp.float32)).astype(jnp.bfloat16)
    prob = expo / tot[..., None]
    dval = jnp.einsum(
        "hrk,rhd->khd", prob.astype(jnp.bfloat16), go3, preferred_element_type=jnp.float32
    )
    dprob = jnp.einsum("rhd,khd->hrk", go3, vals, preferred_element_type=jnp.float32)
    delta = jnp.transpose(jnp.sum(gof * view_out, axis=-1))
    dscore = (prob * (dprob - delta[..., None])).astype(jnp.bfloat16)
    dq_view = jnp.einsum("hrk,khd->rhd", dscore, keys, preferred_element_type=jnp.float32) * inv
    dkey = jnp.einsum("hrk,rhd->khd", dscore, q3, preferred_element_type=jnp.float32) * inv
    dq = (dq_view + dq_time).reshape(rows, inner).astype(jnp.bfloat16)
    dk = (dkey[:rows].reshape(rows, inner) + dk_time).astype(jnp.bfloat16)
    dv = (dval[:rows].reshape(rows, inner) + dv_time).astype(jnp.bfloat16)
    dkc = dkey[rows:].reshape(vt_rows, inner).astype(jnp.bfloat16)
    dvc = dval[rows:].reshape(vt_rows, inner).astype(jnp.bfloat16)
    grad_k = jnp.dot(xn.T, dk, preferred_element_type=jnp.float32) + jnp.dot(
        cn.T, dkc, preferred_element_type=jnp.float32
    )
    grad_v = jnp.dot(xn.T, dv, preferred_element_type=jnp.float32) + jnp.dot(
        cn.T, dvc, preferred_element_type=jnp.float32
    )
    grads = lax.psum_scatter(
        jnp.concatenate([grad_k, grad_v], axis=1), ("dp", "frame"), scatter_dimension=0, tiled=True
    )
    dnorm = jnp.dot(dq, w_query.T, preferred_element_type=jnp.float32)
    dnorm = dnorm + jnp.dot(dk, w_key.T, preferred_element_type=jnp.float32)
    dnorm = dnorm + jnp.dot(dv, w_value.T, preferred_element_type=jnp.float32)
    back = grad_y.astype(jnp.float32) + factor * (
        dnorm - normed * jnp.mean(dnorm * normed, axis=-1, keepdims=True)
    )
    return (block.reshape(latents.shape), back.astype(jnp.bfloat16).reshape(latents.shape), grads)


def solution(mesh):
    return jax.shard_map(
        shards,
        mesh=mesh,
        in_specs=(
            P("dp", "frame", None, None, None),
            P("dp", "frame", None, None, None),
            P("dp", "frame", None, None, None),
            P("dp"),
            P(),
            P(),
            P(),
            P(),
        ),
        out_specs=(
            P("dp", "frame", None, None, None),
            P("dp", "frame", None, None, None),
            P(("dp", "frame"), None),
        ),
        check_vma=False,
    )
```

profile of v0, /device:TPU:2, one launch (start us, length us, event | category | flops | bytes accessed | tf_op | source)
XLA Modules:
  0.0 591.7 jit_solution(16451086971794727714)
XLA Ops:
  9.7 2.0 convolution_convert_fusion.1
  15.5 6.1 %all-to-all-start = ((bf16[16,8,2560]{2,1,0:T(8,128)(2,1)}), bf16[16,8,2560]{2,1,0:T(8,128)(2,1)S(1)}, u32[]{:S(2)}, u32[]{:S(2)}) async-start(bf16[16,8,2560]{2,1,0:T(8,128)(2,1)} %maximum_bitcast_fusion), calls=%async_computation | async-start | bytes 1310720 | tf_op jit(solution)/shard_map/all_to_all | solution.py:104
  22.3 13.2 %all-to-all-done = bf16[16,8,2560]{2,1,0:T(8,128)(2,1)S(1)} async-done(((bf16[16,8,2560]{2,1,0:T(8,128)(2,1)}), bf16[16,8,2560]{2,1,0:T(8,128)(2,1)S(1)}, u32[]{:S(2)}, u32[]{:S(2)}) %all-to-all-start) | async-done | bytes 655392 | tf_op jit(solution)/shard_map/all_to_all | solution.py:104
  37.8 3.1 fusion.46
  40.8 2.1 reshape.152
  42.9 2.0 reshape.148
  44.9 2.2 copy_convert_fusion
  47.1 1.7 fusion.23
  52.1 2.8 copy.91
  54.9 15.8 %fusion = bf16[16,16,8,10,64]{1,4,3,2,0:T(8,128)(2,1)} fusion(f32[16,8,10,16]{3,2,1,0:T(8,128)} %copy.91, f32[16,8,10,64]{3,2,1,0:T(8,128)S(1)} %convert.32), kind=kLoop, calls=%fused_computation.2 | loop fusion | flops 3932160 | bytes 3031040 | tf_op jit(solution)/shard_map/convert_element_type | solution.py:21
  70.7 11.8 %reduce.1 = bf16[16,8,10,64]{0,3,2,1:T(8,128)(2,1)S(1)} reduce(bf16[16,16,8,10,64]{1,4,3,2,0:T(8,128)(2,1)} %fusion, bf16[]{:T(256)} %constant.12.clone.1), dimensions={0}, to_apply=%region_6.7.clone | reduce | flops 1228800 | bytes 2785282 | tf_op jit(solution)/shard_map/reduce_sum | solution.py:52
  85.8 2.0 copy.94
  88.1 14.7 %fusion.1 = bf16[16,16,8,10,64]{1,4,3,2,0:T(8,128)(2,1)} fusion(f32[16,8,10,16]{3,2,1,0:T(8,128)S(1)} %copy.94, f32[16,8,10,64]{3,2,1,0:T(8,128)S(1)} %copy.93), kind=kLoop, calls=%fused_computation.3 | loop fusion | flops 2621440 | bytes 3031040 | tf_op jit(solution)/shard_map/convert_element_type | solution.py:21
  102.8 11.8 %reduce.2 = bf16[16,8,10,64]{0,3,2,1:T(8,128)(2,1)S(1)} reduce(bf16[16,16,8,10,64]{1,4,3,2,0:T(8,128)(2,1)} %fusion.1, bf16[]{:T(256)} %constant.12.clone.1), dimensions={0}, to_apply=%region_7.8.clone | reduce | flops 1228800 | bytes 2785282 | tf_op jit(solution)/shard_map/reduce_sum | solution.py:53
  115.7 2.0 pad_maximum_fusion.1
  117.6 4.3 all-to-all-start.1
  123.4 1.8 copy.77
  125.2 1.7 copy.97
  127.0 8.8 %all-to-all-done.1 = bf16[16,8,2560]{2,1,0:T(8,128)(2,1)} async-done(((bf16[16,8,2560]{2,1,0:T(8,128)(2,1)}), bf16[16,8,2560]{2,1,0:T(8,128)(2,1)}, u32[]{:S(2)}, u32[]{:S(2)}) %all-to-all-start.1) | async-done | bytes 655392 | tf_op jit(solution)/shard_map/all_to_all | solution.py:107
  135.7 2.3 bitcast_convert_fusion
  138.0 137.4 %all-reduce.4.cloned.1.call-done = bf16[16,32,1280]{2,1,0:T(8,128)(2,1)} async-done(((bf16[16,32,1280]{2,1,0:T(8,128)(2,1)}), bf16[16,32,1280]{2,1,0:T(8,128)(2,1)}) %all-reduce.4.cloned.1.call-update) | async-done | bytes 1310736 | tf_op jit(solution)/shard_map/psum | solution.py:12
  278.5 1.8 copy.78
  282.4 1.9 copy.76
  291.8 1.8 copy.99
  293.7 1.9 copy.100
  295.5 2.5 fusion.19
  302.7 3.2 pad_maximum_fusion
  305.9 1.9 copy.98
  307.8 1.9 copy.96
  311.1 2.0 fusion.47
  318.0 264.5 %all-reduce.6.cloned.1.call-done = f32[1280,1280]{0,1:T(8,128)} async-done(((f32[1280,1280]{0,1:T(8,128)}), f32[1280,1280]{0,1:T(8,128)}) %all-reduce.6.cloned.1.call-update) | async-done | bytes 6553616
  582.5 1.5 constant_dynamic-slice_fusion
  (124 shorter events, 42.2 us)
Async XLA Ops:
  7.2 5.0 copy-start
  7.2 4.5 copy-start.5
  9.7 2.5 copy-start.2
  11.7 2.2 copy-start.16
  11.7 1.6 copy-start.6
  11.7 1.6 copy-start.23
  12.1 1.8 copy-start.18
  15.5 20.0 %all-to-all-start = ((bf16[16,8,2560]{2,1,0:T(8,128)(2,1)}), bf16[16,8,2560]{2,1,0:T(8,128)(2,1)S(1)}, u32[]{:S(2)}, u32[]{:S(2)}) async-start(bf16[16,8,2560]{2,1,0:T(8,128)(2,1)} %maximum_bitcast_fusion), calls=%async_computation | async-start | bytes 1310720 | tf_op jit(solution)/shard_map/all_to_all | solution.py:104
  40.8 6.3 %copy-start.10 = (f32[8,10,16,16]{2,3,1,0:T(8,128)S(1)}, f32[8,10,16,16]{2,3,1,0:T(8,128)}, u32[]{:S(2)}) copy-start(f32[8,10,16,16]{2,3,1,0:T(8,128)} %get-tuple-element.28) | copy-start | bytes 245764
  44.9 3.9 copy-start.12
  44.9 3.9 copy-start.29
  44.9 3.9 copy-start.33
  50.2 1.0 copy-start.8
  83.6 1.1 copy-start.31
  84.7 3.1 copy-start.9
  102.8 12.9 %copy-start.27 = (bf16[16,8,640]{2,1,0:T(8,128)(2,1)S(1)}, bf16[16,8,640]{2,1,0:T(8,128)(2,1)}, u32[]{:S(2)}) copy-start(bf16[16,8,640]{2,1,0:T(8,128)(2,1)} %reshape.153) | copy-start | bytes 491524
  102.8 12.9 %copy-start.28 = (bf16[16,8,640]{2,1,0:T(8,128)(2,1)S(1)}, bf16[16,8,640]{2,1,0:T(8,128)(2,1)}, u32[]{:S(2)}) copy-start(bf16[16,8,640]{2,1,0:T(8,128)(2,1)} %reshape.151) | copy-start | bytes 491524
  115.7 6.3 %copy-start.22 = (bf16[1,1,16,32,1280]{4,3,2,1,0:T(8,128)(2,1)S(1)}, bf16[1,1,16,32,1280]{4,3,2,1,0:T(8,128)(2,1)}, u32[]{:S(2)}) copy-start(bf16[1,1,16,32,1280]{4,3,2,1,0:T(8,128)(2,1)} %param.10) | copy-start | bytes 3932164
  117.6 18.1 %all-to-all-start.1 = ((bf16[16,8,2560]{2,1,0:T(8,128)(2,1)}), bf16[16,8,2560]{2,1,0:T(8,128)(2,1)}, u32[]{:S(2)}, u32[]{:S(2)}) async-start(bf16[16,8,2560]{2,1,0:T(8,128)(2,1)} %pad_maximum_fusion.1), calls=%async_computation.1 | async-start | bytes 1310720 | tf_op jit(solution)/shard_map/all_to_all | solution.py:107
  121.9 153.5 %all-reduce.4.cloned.1.call-start = ((), (), s32[]{:S(2)}) async-start(), calls=%async_computation.2 | async-start | bytes 2621440 | tf_op jit(solution)/shard_map/psum | solution.py:12
  123.2 153.3 %copy-start.1 = (bf16[1280,640]{1,0:T(8,128)(2,1)S(1)}, bf16[1280,640]{1,0:T(8,128)(2,1)}, u32[]{:S(2)}) copy-start(bf16[1280,640]{1,0:T(8,128)(2,1)} %param.13) | copy-start | bytes 4915204
  123.2 459.3 %all-reduce.6.cloned.1.call-start = ((), (), s32[]{:S(2)}) async-start(), calls=%async_computation.3 | async-start | bytes 13107200
  275.4 2.4 copy-start.17
  282.4 3.3 copy-start.34
  285.7 1.0 copy-start.32
  288.5 1.8 copy-start.13
  295.5 2.5 copy-start.3
  299.6 1.6 copy-start.25
  309.6 3.5 copy-start.15
  314.1 1.1 copy-start.30
  314.1 1.6 copy-start.7
  315.2 1.8 copy-start.24
  (7 other events, 6.0 us)
Sparse Core Ops, SparseCore 0:
  125.4 149.9 all-reduce.3
  306.0 276.4 all-reduce.5
where the time goes:
time: 593 us; the launch traced here: 592 us
  waiting for transfers between devices  424 us (72%)
  other arithmetic  76.1 us (13%)
  local copies, waits for them, and re-layouts  40.9 us (7%)
  matrix products  25.1 us (4%)
  between operations  15.1 us (3%)
  starting transfers between devices  10.7 us (2%)
    unnamed x3, waiting for transfers between devices  265 us
    psum x1, waiting for transfers between devices, broadcast(): return lax.psum(kept, axis)  137 us
    convert_element_type x2, other arithmetic, to_half(): tensor.astype(jnp.bfloat16)  30.6 us
    all_to_all x1, waiting for transfers between devices, shards(): lax.all_to_all(packed, 'frame', split_axis=0, concat_axis=0, tiled=True)  13.2 us
  transfers between devices with their start and end apart: 4, of which 4 were waited for; matrix products, arithmetic and copies ran while one was open for 3% of the time, Pallas kernels for 0%

commit v1 on v0

v1 whole, which is shorter than its diff:
```python
import jax
import jax.numpy as jnp
from jax import lax
from jax.experimental import pallas as pl
from jax.experimental.pallas import tpu as pltpu
from jax.sharding import PartitionSpec as P

MESH = pl.DeviceIdType.MESH
BF = jnp.bfloat16
F32 = jnp.float32
D, INNER, HD = 1280, 640, 64
ROWS, VT, NF = 128, 32, 16
KEYS = 256
EPS = 1e-6
CHUNKS = ((0, 2), (2, 5))
NC = len(CHUNKS)


def nn(a, b):
    return jnp.dot(a, b, preferred_element_type=F32)


def nt(a, b):
    return lax.dot_general(a, b, (((1,), (1,)), ((), ())), preferred_element_type=F32)


def tn(a, b):
    return lax.dot_general(a, b, (((0,), (0,)), ((), ())), preferred_element_type=F32)


def attend(q, k, v, go, mask):
    lane = lax.broadcasted_iota(jnp.int32, (1, 128), 1)
    first = (lane < HD).astype(F32).astype(BF)
    second = (lane >= HD).astype(F32).astype(BF)
    qm = jnp.concatenate([q * first, q * second], axis=0)
    gm = jnp.concatenate([go * first, go * second], axis=0)
    km = jnp.concatenate([k * first, k * second], axis=0)
    vm = jnp.concatenate([v * first, v * second], axis=0)
    e = jnp.where(mask, jnp.exp(nt(qm, k) * 0.125), 0.0)
    dp = nt(gm, v)
    r = 1.0 / jnp.sum(e, axis=1, keepdims=True)
    eb = e.astype(BF)
    o = nn(jnp.concatenate([eb[:ROWS], eb[ROWS:]], axis=1), vm)
    o = o * jnp.where(lane < HD, r[:ROWS], r[ROWS:])
    delta = jnp.sum(gm.astype(F32) * jnp.concatenate([o, o], axis=0), axis=1, keepdims=True)
    p = e * r
    ds = (p * (dp - delta)).astype(BF)
    dq = nn(jnp.concatenate([ds[:ROWS], ds[ROWS:]], axis=1), km) * 0.125
    dk = tn(ds, qm) * 0.125
    dv = tn(p.astype(BF), gm)
    return o, dq, dk, dv


def pack(top, bottom):
    return jnp.concatenate([top.reshape(NF, 8, 128), bottom.reshape(NF, 8, 128)], axis=1).astype(BF)


def unpack(block):
    wide = block.astype(F32)
    return wide[:, :8].reshape(ROWS, 128), wide[:, 8:].reshape(ROWS, 128)


def kernel(
    lat, ogr, vid, own, wq_h, wk_h, wv_h, wo_h,
    block_h, back_h, grad_o,
    lat_v, ogr_v, wq, wk, wv, wo, block_v, back_v,
    normed, xc, q_v, kk, vv, go_v, snd, rcv, snd2, rcv2,
    va, vb, vs, vy, v2, vx,
    ov, dqv, dkv_v, dvv_v, h_v, dq_b, dkv,
    pt, gx, gy, rx, ry, s2x, s2y, r2x, r2y, m1, s3, r3,
    load_sem, as1, ar1, as2, ar2, ms, mr,
):
    dp = lax.axis_index("dp")
    me = lax.axis_index("frame")
    z, x_lo = dp // 2, dp % 2
    x_hi, y, c = me // 8, (me // 2) % 4, me % 2
    x = x_hi * 2 + x_lo

    def at_x(d):
        to = (x + d) % 4
        return (z * 2 + to % 2, (to // 2) * 8 + y * 2 + c)

    def at_y(d):
        return (dp, x_hi * 8 + ((y + d) % 4) * 2 + c)

    def at_z(d):
        return (((z + d) % 8) * 2 + x_lo, me)

    def at_f(d):
        return (dp, (me + d) % NF)

    pair = (dp, me + 1 - 2 * c)

    loads = [
        pltpu.make_async_copy(src, dst, load_sem.at[i])
        for i, (src, dst) in enumerate(
            [(lat, lat_v), (wq_h, wq), (wk_h, wk), (wv_h, wv), (ogr, ogr_v), (wo_h, wo), (vid.at[:, c], va)]
        )
    ]
    for copy in loads:
        copy.start()

    barrier = pltpu.get_barrier_semaphore()
    peers = [at_f(d) for d in range(1, NF)] + [at_x(1), at_x(3)] + [at_z(d) for d in range(1, 8)]
    for peer in peers:
        pl.semaphore_signal(barrier, inc=1, device_id=peer, device_id_type=MESH)

    count = [0]
    started = []

    def send(src, dst, peer, ss=None, rs=None):
        if ss is None:
            ss, rs = ms.at[count[0]], mr.at[count[0]]
            count[0] += 1
        copy = pltpu.make_async_remote_copy(
            src_ref=src, dst_ref=dst, send_sem=ss, recv_sem=rs, device_id=peer, device_id_type=MESH
        )
        copy.start()
        started.append(copy)
        return copy

    def arrived(dst, rs):
        pltpu.make_async_remote_copy(
            src_ref=dst, dst_ref=dst, send_sem=rs, recv_sem=rs, device_id=pair, device_id_type=MESH
        ).wait_recv()

    loads[0].wait()
    xf = lat_v[...].astype(F32)
    factor = lax.rsqrt(jnp.mean(xf * xf, axis=1, keepdims=True) + EPS)
    norm = xf * factor
    normed[...] = norm
    xn = norm.astype(BF)
    xc[0, :ROWS] = xn

    pl.semaphore_wait(barrier, len(peers))
    core_copy = send(vid.at[:, 1 - c], vb, pair)
    xn_copy = send(xc.at[0, pl.ds(0, ROWS)], xc.at[1, pl.ds(0, ROWS)], pair)

    for copy in loads[1:6]:
        copy.wait()
    grad_y = ogr_v[...]
    for n, (a, b) in enumerate(CHUNKS):
        cols = slice(a * 128, b * 128)
        qf = nn(xn, wq[:, cols])
        kf = nn(xn, wk[:, cols])
        vf = nn(xn, wv[:, cols])
        gf = nt(grad_y, wo[cols, :])
        for p in range(a, b):
            part = slice((p - a) * 128, (p - a + 1) * 128)
            snd[:, :, p * 256 : p * 256 + 128] = pack(qf[:, part], vf[:, part])
            snd[:, :, p * 256 + 128 : p * 256 + 256] = pack(kf[:, part], gf[:, part])
        lanes = pl.ds(a * 256, (b - a) * 256)
        for d in range(1, NF):
            to = (me + d) % NF
            send(snd.at[to, :, lanes], rcv.at[me, :, lanes], at_f(d), as1.at[n, d], ar1.at[n, d])
        q_v[:, cols] = qf.astype(BF)
        kk[:ROWS, cols] = kf.astype(BF)
        vv[:ROWS, cols] = vf.astype(BF)
        go_v[:, cols] = gf.astype(BF)
    rcv[me] = snd[me]

    who = own[0]
    loads[6].wait()
    core_copy.wait_recv()
    w = (who % 2 == c).astype(F32)
    vs[...] = (va[...].astype(F32) * w + vb[...].astype(F32) * (1.0 - w)).astype(BF).reshape(2, 4, VT, D)
    y_copies = [send(vs.at[:, (y + d) % 4], vy.at[d - 1], at_y(d)) for d in range(1, 4)]

    new = lax.broadcasted_iota(jnp.int32, (INNER, 1), 0)
    u = (new * 52429) >> 18
    k5 = new - 5 * u
    uz, lo, hi = u & 7, (u >> 3) & 3, u >> 5
    column = lax.broadcasted_iota(jnp.int32, (1, D), 1)

    def one_hot(ux, uy):
        old = ((((uz * 2 + (ux & 1)) * 2 + (ux >> 1)) * 4 + uy) * 2 + c) * 5 + k5
        return (old == column).astype(F32).astype(BF)

    pt[0] = one_hot(hi, lo)
    pt[1] = one_hot(lo, hi)
    xn_copy.wait_recv()

    same = (
        (lax.broadcasted_iota(jnp.int32, (2 * ROWS, ROWS), 0) - lax.broadcasted_iota(jnp.int32, (2 * ROWS, ROWS), 1)) & 7
    ) == 0
    for n, (a, b) in enumerate(CHUNKS):
        lanes = pl.ds(a * 256, (b - a) * 256)
        for d in range(1, NF):
            arrived(rcv.at[(me + NF - d) % NF, :, lanes], ar1.at[n, d])
        for p in range(a, b):
            q, v = unpack(rcv[:, :, p * 256 : p * 256 + 128])
            k, go = unpack(rcv[:, :, p * 256 + 128 : p * 256 + 256])
            o, dq, dk, dv = attend(q.astype(BF), k.astype(BF), v.astype(BF), go.astype(BF), same)
            snd2[:, :, p * 256 : p * 256 + 128] = pack(o, dk)
            snd2[:, :, p * 256 + 128 : p * 256 + 256] = pack(dq, dv)
        for d in range(1, NF):
            to = (me + d) % NF
            send(snd2.at[to, :, lanes], rcv2.at[me, :, lanes], at_f(d), as2.at[n, d], ar2.at[n, d])
        if n == 0:
            oy = (who // 2) % 4
            total = vs[:, y].astype(F32) * (oy == y).astype(F32)
            for d in range(1, 4):
                y_copies[d - 1].wait_recv()
                total = total + vy[d - 1].astype(F32) * (oy == (y + 4 - d) % 4).astype(F32)
            v2[...] = total.astype(BF)
            x_copy = send(v2.at[1 - x_hi], vx, (dp, (1 - x_hi) * 8 + y * 2 + c))
    rcv2[me] = snd2[me]

    x_copy.wait_recv()
    w = (who // 8 == x_hi).astype(F32)
    cond = v2[x_hi].astype(F32) * w + vx[...].astype(F32) * (1.0 - w)
    cn = (cond * lax.rsqrt(jnp.mean(cond * cond, axis=1, keepdims=True) + EPS)).astype(BF)
    xc[0, ROWS:] = cn
    cn_copy = send(xc.at[0, pl.ds(ROWS, VT)], xc.at[1, pl.ds(ROWS, VT)], pair)
    zeros = jnp.zeros((KEYS - ROWS - VT, INNER), BF)
    kk[ROWS : ROWS + VT] = nn(cn, wk[...]).astype(BF)
    vv[ROWS : ROWS + VT] = nn(cn, wv[...]).astype(BF)
    kk[ROWS + VT :] = zeros
    vv[ROWS + VT :] = zeros

    real = lax.broadcasted_iota(jnp.int32, (2 * ROWS, KEYS), 1) < ROWS + VT
    for p in range(5):
        cols = slice(p * 128, (p + 1) * 128)
        o, dq, dk, dv = attend(q_v[:, cols], kk[:, cols], vv[:, cols], go_v[:, cols], real)
        ov[:, cols] = o
        dqv[:, cols] = dq
        dkv_v[:, cols] = dk[: ROWS + VT]
        dvv_v[:, cols] = dv[: ROWS + VT]

    cn_copy.wait_recv()
    both = xc[...].reshape(2 * (ROWS + VT), D)
    xnp = [nt(pt[i], both).astype(BF) for i in range(2)]
    pt[0, :, : 2 * (ROWS + VT)] = xnp[0]
    pt[1, :, : 2 * (ROWS + VT)] = xnp[1]

    for n, (a, b) in enumerate(CHUNKS):
        lanes = pl.ds(a * 256, (b - a) * 256)
        for d in range(1, NF):
            arrived(rcv2.at[(me + NF - d) % NF, :, lanes], ar2.at[n, d])
        for p in range(a, b):
            cols = slice(p * 128, (p + 1) * 128)
            vcols = slice(INNER + p * 128, INNER + (p + 1) * 128)
            o, dk = unpack(rcv2[:, :, p * 256 : p * 256 + 128])
            dq, dv = unpack(rcv2[:, :, p * 256 + 128 : p * 256 + 256])
            h_v[:, cols] = (ov[:, cols] + o).astype(BF)
            dq_b[:, cols] = (dqv[:, cols] + dq).astype(BF)
            dkv[0, :ROWS, cols] = (dkv_v[:ROWS, cols] + dk).astype(BF)
            dkv[0, :ROWS, vcols] = (dvv_v[:ROWS, cols] + dv).astype(BF)
    dkv[0, ROWS:, :INNER] = dkv_v[ROWS:].astype(BF)
    dkv[0, ROWS:, INNER:] = dvv_v[ROWS:].astype(BF)
    dkv_copy = send(dkv.at[0], dkv.at[1], pair)
    dkv_copy.wait_recv()

    deep = 2 * (ROWS + VT)
    rhs = dkv[...].reshape(deep, D)
    xs, ys = [], []
    for d in (1, 2, 3, 0):
        bx = pl.multiple_of(((x + d) % 4) * 160, 32)
        gx[d] = nn(pt[0, pl.ds(bx, 160), :deep], rhs[:, :INNER]).astype(BF)
        if d:
            xs.append(send(gx.at[d], rx.at[d - 1], at_x(d)))
        by = pl.multiple_of(((y + d) % 4) * 160, 32)
        gy[d] = nn(pt[1, pl.ds(by, 160), :deep], rhs[:, INNER:]).astype(BF)
        if d:
            ys.append(send(gy.at[d], ry.at[d - 1], at_y(d)))

    block_v[...] = (lat_v[...].astype(F32) + nn(h_v[...], wo[...])).astype(BF)
    block_out = pltpu.make_async_copy(block_v, block_h, load_sem.at[7])
    block_out.start()
    mine = dkv[0, :ROWS]
    dn = nt(dq_b[...], wq[...]) + nt(mine[:, :INNER], wk[...]) + nt(mine[:, INNER:], wv[...])
    norm = normed[...]
    xf = lat_v[...].astype(F32)
    factor = lax.rsqrt(jnp.mean(xf * xf, axis=1, keepdims=True) + EPS)
    back = ogr_v[...].astype(F32) + factor * (dn - norm * jnp.mean(dn * norm, axis=1, keepdims=True))
    back_v[...] = back.astype(BF)
    back_out = pltpu.make_async_copy(back_v, back_h, load_sem.at[8])
    back_out.start()

    pad = jnp.zeros((8, INNER), F32)

    def first_sum(g, r, copies, at):
        total = g[0].astype(F32)
        for d in range(1, 4):
            copies[d - 1].wait_recv()
            total = total + r[d - 1].astype(F32)
        m1[at] = total

    def second_send(at, position, s2, r2, peer):
        copies = []
        for d in range(1, 4):
            rows = pl.multiple_of(((position + d) % 4) * 40, 8)
            s2[d] = jnp.concatenate([m1[at, pl.ds(rows, 40), :], pad], axis=0).astype(BF)
            copies.append(send(s2.at[d], r2.at[d - 1], peer(d)))
        return copies

    def second_sum(at, position, r2, copies):
        total = m1[at, pl.ds(pl.multiple_of(position * 40, 8), 40), :]
        for d in range(1, 4):
            copies[d - 1].wait_recv()
            total = total + r2[d - 1].astype(F32)[:40]
        return total.astype(BF)

    first_sum(gx, rx, xs, 0)
    x2 = second_send(0, y, s2x, r2x, at_y)
    first_sum(gy, ry, ys, 1)
    y2 = second_send(1, x, s2y, r2y, at_x)

    slot = lax.broadcasted_iota(jnp.int32, (128, 1), 0)
    sz, sk = slot >> 4, slot & 7
    source = jnp.where(sk < 5, ((slot >> 3) & 1) * 40 + sz * 5 + sk, -1)
    place = (source == lax.broadcasted_iota(jnp.int32, (1, 80), 1)).astype(F32).astype(BF)
    tx = second_sum(0, y, r2x, x2)
    ty = second_sum(1, x, r2y, y2)
    s3[...] = nn(place[:, :40], tx).astype(BF).reshape(8, 16, INNER) + nn(place[:, 40:], ty).astype(BF).reshape(
        8, 16, INNER
    )
    zs = [send(s3.at[(z + d) % 8], r3.at[d - 1], at_z(d)) for d in range(1, 8)]
    total = s3[z].astype(F32)
    for d in range(1, 8):
        zs[d - 1].wait_recv()
        total = total + r3[d - 1].astype(F32)
    grad_o[:, :INNER] = total[:5]
    grad_o[:, INNER:] = total[8:13]

    block_out.wait()
    back_out.wait()
    for copy in started:
        copy.wait_send()


def shards(latents, out_grad, video, owner, w_query, w_key, w_value, w_out):
    hbm = pl.BlockSpec(memory_space=pl.ANY)
    span = ROWS + VT
    vm = pltpu.VMEM
    dma = pltpu.SemaphoreType.DMA
    half = ((ROWS, INNER), BF)
    scratch = [
        vm((ROWS, D), BF), vm((ROWS, D), BF),
        vm((D, INNER), BF), vm((D, INNER), BF), vm((D, INNER), BF), vm((INNER, D), BF),
        vm((ROWS, D), BF), vm((ROWS, D), BF),
        vm((ROWS, D), F32), vm((2, span, D), BF),
        vm(*half), vm((KEYS, INNER), BF), vm((KEYS, INNER), BF), vm(*half),
        vm((NF, 16, D), BF), vm((NF, 16, D), BF), vm((NF, 16, D), BF), vm((NF, 16, D), BF),
        vm((8, VT, D), BF), vm((8, VT, D), BF), vm((2, 4, VT, D), BF), vm((3, 2, VT, D), BF),
        vm((2, VT, D), BF), vm((VT, D), BF),
        vm((ROWS, INNER), F32), vm((ROWS, INNER), F32), vm((span, INNER), F32), vm((span, INNER), F32),
        vm(*half), vm(*half), vm((2, span, D), BF),
        vm((2, INNER, D), BF),
        vm((4, 160, INNER), BF), vm((4, 160, INNER), BF), vm((3, 160, INNER), BF), vm((3, 160, INNER), BF),
        vm((4, 48, INNER), BF), vm((4, 48, INNER), BF), vm((3, 48, INNER), BF), vm((3, 48, INNER), BF),
        vm((2, 160, INNER), F32), vm((8, 16, INNER), BF), vm((7, 16, INNER), BF),
        dma((9,)), dma((NC, NF)), dma((NC, NF)), dma((NC, NF)), dma((NC, NF)), dma((32,)), dma((32,)),
    ]
    block, back, grads = pl.pallas_call(
        kernel,
        out_shape=(
            jax.ShapeDtypeStruct((ROWS, D), BF),
            jax.ShapeDtypeStruct((ROWS, D), BF),
            jax.ShapeDtypeStruct((5, D), F32),
        ),
        in_specs=[hbm, hbm, hbm, pl.BlockSpec(memory_space=pltpu.SMEM)] + [hbm] * 4,
        out_specs=(hbm, hbm, pl.BlockSpec(memory_space=pltpu.VMEM)),
        scratch_shapes=scratch,
        compiler_params=pltpu.CompilerParams(
            collective_id=0, has_side_effects=True, vmem_limit_bytes=48 * 1024 * 1024
        ),
    )(
        latents.reshape(ROWS, D),
        out_grad.reshape(ROWS, D),
        video.reshape(8, 2, VT, D),
        owner,
        w_query,
        w_key,
        w_value,
        w_out,
    )
    return block.reshape(latents.shape), back.reshape(latents.shape), grads


def solution(mesh):
    tokens = P("dp", "frame", None, None, None)
    return jax.shard_map(
        shards,
        mesh=mesh,
        in_specs=(tokens, tokens, tokens, P("dp"), P(), P(), P(), P()),
        out_specs=(tokens, tokens, P(("dp", "frame"), None)),
        check_vma=False,
    )
```

time: 593 us -> 76.5 us (0.13)
  waiting for transfers between devices: 424 us -> 0 us
  other arithmetic: 76.1 us -> 0 us
  Pallas kernels: 0 us -> 66.8 us
  local copies, waits for them, and re-layouts: 40.9 us -> 8.18 us
  matrix products: 25.1 us -> 0 us
  between operations: 15.1 us -> 1.3 us
  starting transfers between devices: 10.7 us -> 0 us
    unnamed x3 -> x0, waiting for transfers between devices: 265 us -> none
    psum x1 -> x0, waiting for transfers between devices: 137 us -> none  [broadcast(): return lax.psum(kept, axis)]
    pallas_call x0 -> x1, Pallas kernels: none -> 66.8 us  [shards(): pl.pallas_call(kernel, out_shape=(jax.ShapeDtypeStruct((ROWS, D), BF), ja...]
    convert_element_type x7 -> x0, other arithmetic: 37.4 us -> none  [the longest x2 30.6 us: to_half(): tensor.astype(jnp.bfloat16)]
    reduce_sum x4 -> x0, other arithmetic: 25.9 us -> none  [the longest x1 11.8 us: frame_local(): jnp.sum(to_half(jnp.einsum('nhfg,fnhd->fgnhd', tprob, grad_f)), axis=0)]
    dot_general x24 -> x0, matrix products: 25.1 us -> none  [the longest x1 3.05 us: frame_local(): jnp.einsum('fnhd,gnhd->nhfg', query, key, preferred_element_type=jnp.floa...]
    all_to_all x2 -> x0, waiting for transfers between devices: 21.9 us -> none  [the longest x1 13.2 us: shards(): lax.all_to_all(packed, 'frame', split_axis=0, concat_axis=0, tiled=True)]
    reshape x10 -> x0, local copies, waits for them, and re-layouts: 13.4 us -> none  [the longest x1 2.09 us: frame_local(): grad_o = piece[:, :, 3 * inner:].reshape(shaped)]
  transfers between devices with their start and end apart: 4 -> 0, of which waited for: 4 -> 0; matrix products, arithmetic and copies ran while one was open for 3% -> 0% of each run, Pallas kernels for 0% -> 0%
where the time goes in v1:
time: 76.5 us; the launch traced here: 76.3 us
  Pallas kernels  66.8 us (87%)
  local copies, waits for them, and re-layouts  8.18 us (11%)
  between operations  1.3 us (2%)
    pallas_call x1, Pallas kernels, shards(): pl.pallas_call(kernel, out_shape=(jax.ShapeDtypeStruct((ROWS, D), BF), ja...  66.8 us
    unnamed x13, local copies, waits for them, and re-layouts  8.18 us

profile of v1, /device:TPU:2, one launch (start us, length us, event | category | flops | bytes accessed | tf_op | source)
XLA Modules:
  0.0 76.3 jit_solution(17761669786073454266)
XLA Ops:
  1.3 0.0 copy-start
  1.3 1.4 %copy-done = bf16[1280,640]{1,0:T(8,128)(2,1)S(1)} copy-done((bf16[1280,640]{1,0:T(8,128)(2,1)S(1)}, bf16[1280,640]{1,0:T(8,128)(2,1)}, u32[]{:S(2)}) %copy-start) | copy-done | bytes 1638424
  2.7 0.0 copy-start.1
  2.7 1.4 %copy-done.1 = bf16[1280,640]{1,0:T(8,128)(2,1)S(1)} copy-done((bf16[1280,640]{1,0:T(8,128)(2,1)S(1)}, bf16[1280,640]{1,0:T(8,128)(2,1)}, u32[]{:S(2)}) %copy-start.1) | copy-done | bytes 1638424
  4.1 0.0 copy-start.2
  4.1 1.3 %copy-done.2 = bf16[1,1,16,32,1280]{4,3,2,1,0:T(8,128)(2,1)S(1)} copy-done((bf16[1,1,16,32,1280]{4,3,2,1,0:T(8,128)(2,1)S(1)}, bf16[1,1,16,32,1280]{4,3,2,1,0:T(8,128)(2,1)}, u32[]{:S(2)}) %copy-start.2) | copy-done | bytes 1310744
  5.5 0.0 copy-start.3
  5.5 1.0 %copy-done.3 = bf16[1,1,8,16,1280]{4,3,2,1,0:T(8,128)(2,1)S(1)} copy-done((bf16[1,1,8,16,1280]{4,3,2,1,0:T(8,128)(2,1)S(1)}, bf16[1,1,8,16,1280]{4,3,2,1,0:T(8,128)(2,1)}, u32[]{:S(2)}) %copy-start.3) | copy-done | bytes 327704
  6.4 0.0 copy-start.4
  6.4 1.0 %copy-done.4 = bf16[1,1,8,16,1280]{4,3,2,1,0:T(8,128)(2,1)S(1)} copy-done((bf16[1,1,8,16,1280]{4,3,2,1,0:T(8,128)(2,1)S(1)}, bf16[1,1,8,16,1280]{4,3,2,1,0:T(8,128)(2,1)}, u32[]{:S(2)}) %copy-start.4) | copy-done | bytes 327704
  7.4 66.8 %shard_map.103 = (bf16[128,1280]{1,0:T(8,128)(2,1)S(1)}, bf16[128,1280]{1,0:T(8,128)(2,1)S(1)}, f32[5,1280]{1,0:T(8,128)S(1)}) custom-call(bf16[128,1280]{1,0:T(8,128)(2,1)S(1)} %bitcast.6, bf16[128,1280]{1,0:T(8,128)(2,1)S(1)} %bitcast.7, bf16[8,2,32,1280]{3,2,1,0:T(8,128)(2,1)S(1)} %bitcast.5, s32[1]{0:T(128)S(6)} %copy.14.own, ...), custom_call_target="tpu_custom_call" | custom-call | tf_op jit(solution)/shard_map/pallas_call | solution.py:355
  74.2 0.7 copy.15
  74.9 0.7 copy.16
  75.7 0.6 copy.17
Async XLA Ops:
  1.3 1.4 %copy-start = (bf16[1280,640]{1,0:T(8,128)(2,1)S(1)}, bf16[1280,640]{1,0:T(8,128)(2,1)}, u32[]{:S(2)}) copy-start(bf16[1280,640]{1,0:T(8,128)(2,1)} %wq_h.1) | copy-start | bytes 4915204
  2.7 1.4 %copy-start.1 = (bf16[1280,640]{1,0:T(8,128)(2,1)S(1)}, bf16[1280,640]{1,0:T(8,128)(2,1)}, u32[]{:S(2)}) copy-start(bf16[1280,640]{1,0:T(8,128)(2,1)} %wk_h.1) | copy-start | bytes 4915204
  4.1 1.3 %copy-start.2 = (bf16[1,1,16,32,1280]{4,3,2,1,0:T(8,128)(2,1)S(1)}, bf16[1,1,16,32,1280]{4,3,2,1,0:T(8,128)(2,1)}, u32[]{:S(2)}) copy-start(bf16[1,1,16,32,1280]{4,3,2,1,0:T(8,128)(2,1)} %param.10) | copy-start | bytes 3932164
  5.5 1.0 %copy-start.3 = (bf16[1,1,8,16,1280]{4,3,2,1,0:T(8,128)(2,1)S(1)}, bf16[1,1,8,16,1280]{4,3,2,1,0:T(8,128)(2,1)}, u32[]{:S(2)}) copy-start(bf16[1,1,8,16,1280]{4,3,2,1,0:T(8,128)(2,1)} %param.8) | copy-start | bytes 983044
  6.4 1.0 %copy-start.4 = (bf16[1,1,8,16,1280]{4,3,2,1,0:T(8,128)(2,1)S(1)}, bf16[1,1,8,16,1280]{4,3,2,1,0:T(8,128)(2,1)}, u32[]{:S(2)}) copy-start(bf16[1,1,8,16,1280]{4,3,2,1,0:T(8,128)(2,1)} %param.9) | copy-start | bytes 983044

commit v2 on v1

v2 whole, which is shorter than its diff:
```python
import jax
import jax.numpy as jnp
from jax import lax
from jax.experimental import pallas as pl
from jax.experimental.pallas import tpu as pltpu
from jax.sharding import PartitionSpec as P

MESH = pl.DeviceIdType.MESH
BF = jnp.bfloat16
F32 = jnp.float32
D, INNER, HD = 1280, 640, 64
ROWS, VT, NF = 128, 32, 16
KEYS = 256
EPS = 1e-6
CHUNKS = ((0, 3), (3, 5))
TURNS = (8, 7, 9, 6, 10, 5, 11, 4, 12, 3, 13, 2, 14, 1, 15)
SLOTS = (4, 3, 5, 2, 6, 1, 7, 0)
ORDER = (2, 1, 3)
FAR = (4, 3, 5, 2, 6, 1, 7)


def nn(a, b):
    return jnp.dot(a, b, preferred_element_type=F32)


def nt(a, b):
    return lax.dot_general(a, b, (((1,), (1,)), ((), ())), preferred_element_type=F32)


def tn(a, b):
    return lax.dot_general(a, b, (((0,), (0,)), ((), ())), preferred_element_type=F32)


def attend(q, k, v, go, mask):
    lane = lax.broadcasted_iota(jnp.int32, (1, 128), 1)
    first = (lane < HD).astype(F32).astype(BF)
    second = (lane >= HD).astype(F32).astype(BF)
    qm = jnp.concatenate([q * first, q * second], axis=0)
    gm = jnp.concatenate([go * first, go * second], axis=0)
    km = jnp.concatenate([k * first, k * second], axis=0)
    vm = jnp.concatenate([v * first, v * second], axis=0)
    e = jnp.where(mask, jnp.exp(nt(qm, k) * 0.125), 0.0)
    dp = nt(gm, v)
    r = 1.0 / jnp.sum(e, axis=1, keepdims=True)
    eb = e.astype(BF)
    o = nn(jnp.concatenate([eb[:ROWS], eb[ROWS:]], axis=1), vm)
    o = o * jnp.where(lane < HD, r[:ROWS], r[ROWS:])
    delta = jnp.sum(gm.astype(F32) * jnp.concatenate([o, o], axis=0), axis=1, keepdims=True)
    p = e * r
    ds = (p * (dp - delta)).astype(BF)
    dq = nn(jnp.concatenate([ds[:ROWS], ds[ROWS:]], axis=1), km) * 0.125
    dk = tn(ds, qm) * 0.125
    dv = tn(p.astype(BF), gm)
    return o, dq, dk, dv


def fold(left, right):
    n, m = left.shape[1], right.shape[1]
    if m < n:
        right = jnp.concatenate([right, jnp.zeros((ROWS, n - m), F32)], axis=1)
    return jnp.concatenate([left.reshape(NF, 8, n), right.reshape(NF, 8, n)], axis=1).astype(BF)


def unfold(block, m):
    wide = block.astype(F32)
    n = wide.shape[2]
    return jnp.concatenate([wide[:, :8].reshape(ROWS, n), wide[:, 8:, :m].reshape(ROWS, m)], axis=1)


def kernel(
    lat, ogr, vid, own, wq_h, wk_h, wv_h, wo_h,
    block_h, back_h, grad_o,
    lat_v, ogr_v, wq, wk, wv, wo, block_v, back_v, grad_v,
    normed, xt, q_v, kk, vv, go_v, sx, sg, ax, ag, so, sd, ro, rd,
    va, vb, vs, vr, ov, dqv, dqt, dkv,
    pt, xp, gx, gy, rx, ry, s2x, s2y, r2x, r2y, m1, s3, r3,
    load_sem, as1, ar1, as2, ar2, ms, mr,
):
    dp = lax.axis_index("dp")
    me = lax.axis_index("frame")
    z, x_lo = dp // 2, dp % 2
    x_hi, y, c = me // 8, (me // 2) % 4, me % 2
    x = x_hi * 2 + x_lo

    def at_x(d):
        to = (x + d) % 4
        return (z * 2 + to % 2, (to // 2) * 8 + y * 2 + c)

    def at_y(d):
        return (dp, x_hi * 8 + ((y + d) % 4) * 2 + c)

    def at_z(d):
        return (((z + d) % 8) * 2 + x_lo, me)

    def at_f(d):
        return (dp, (me + d) % NF)

    pair = (dp, me + 1 - 2 * c)

    loads = [
        pltpu.make_async_copy(src, dst, load_sem.at[i])
        for i, (src, dst) in enumerate(
            [(lat, lat_v), (ogr, ogr_v), (wo_h, wo), (wq_h, wq), (wk_h, wk), (wv_h, wv), (vid.at[:, c], va)]
        )
    ]
    loads[0].start()

    barrier = pltpu.get_barrier_semaphore()
    peers = [at_f(d) for d in range(1, NF)] + [at_x(1), at_x(3)] + [at_z(d) for d in range(1, 8)]
    for peer in peers:
        pl.semaphore_signal(barrier, inc=1, device_id=peer, device_id_type=MESH)
    for copy in loads[1:]:
        copy.start()

    count = [0]
    started = []

    def send(src, dst, peer, ss=None, rs=None):
        if ss is None:
            ss, rs = ms.at[count[0]], mr.at[count[0]]
            count[0] += 1
        copy = pltpu.make_async_remote_copy(
            src_ref=src, dst_ref=dst, send_sem=ss, recv_sem=rs, device_id=peer, device_id_type=MESH
        )
        copy.start()
        started.append(copy)
        return copy

    def scatter(src, dst, ss, rs):
        for d in TURNS:
            send(src.at[(me + d) % NF], dst.at[me], at_f(d), ss.at[d], rs.at[d])

    def gathered(src, dst, rs):
        dst[me] = src[me]
        for d in TURNS:
            slot = dst.at[(me + NF - d) % NF]
            pltpu.make_async_remote_copy(
                src_ref=slot, dst_ref=slot, send_sem=rs.at[d], recv_sem=rs.at[d], device_id=pair, device_id_type=MESH
            ).wait_recv()

    def to_pair(ref, row, rows, cols=None):
        if cols is None:
            return send(ref.at[pl.ds(row, rows)], ref.at[pl.ds(row + rows, rows)], pair)
        return send(ref.at[:, pl.ds(row, rows), cols], ref.at[:, pl.ds(row + rows, rows), cols], pair)

    loads[0].wait()
    xf = lat_v[...].astype(F32)
    factor = lax.rsqrt(jnp.mean(xf * xf, axis=1, keepdims=True) + EPS)
    norm = xf * factor
    normed[...] = norm
    xt[:ROWS] = norm.astype(BF)
    sx[...] = fold(norm[:, :INNER], norm[:, INNER:])
    loads[1].wait()
    loads[2].wait()
    gf = nt(ogr_v[...], wo[...])
    sg[...] = fold(gf[:, :384], gf[:, 384:])
    go_v[...] = gf.astype(BF)

    pl.semaphore_wait(barrier, len(peers))
    core_copies = [send(vid.at[(me // 2 + d) % 8, 1 - c], vb.at[d], pair) for d in SLOTS]
    scatter(sx, ax, as1.at[0], ar1.at[0])
    scatter(sg, ag, as1.at[1], ar1.at[1])
    xn_copy = to_pair(xt, 0, ROWS)

    for copy in loads[3:6]:
        copy.wait()
    xn = xt[:ROWS]
    q_v[...] = nn(xn, wq[...]).astype(BF)
    kk[:ROWS] = nn(xn, wk[...]).astype(BF)
    vv[:ROWS] = nn(xn, wv[...]).astype(BF)

    who = own[0]
    loads[6].wait()
    w = (who % 2 == c).astype(F32)
    video_copies = {}
    for copy, d in zip(core_copies, SLOTS):
        copy.wait_recv()
        to = (me // 2 + d) % 8
        vs[d] = (va[to].astype(F32) * w + vb[d].astype(F32) * (1.0 - w)).astype(BF)
        if d:
            video_copies[d] = send(vs.at[d], vr.at[d], (dp, to * 2 + c))

    new = lax.broadcasted_iota(jnp.int32, (INNER, 1), 0)
    u = (new * 52429) >> 18
    k5 = new - 5 * u
    uz, lo, hi = u & 7, (u >> 3) & 3, u >> 5
    column = lax.broadcasted_iota(jnp.int32, (1, D), 1)

    def one_hot(ux, uy):
        old = ((((uz * 2 + (ux & 1)) * 2 + (ux >> 1)) * 4 + uy) * 2 + c) * 5 + k5
        return (old == column).astype(F32).astype(BF)

    pt[0] = one_hot(hi, lo)
    pt[1] = one_hot(lo, hi)

    def permute(first, last):
        rows = xt[first:last]
        for i in range(2):
            xp[i, :, first:last] = nt(pt[i], rows).astype(BF)

    gathered(sx, ax, ar1.at[0])
    xa = unfold(ax[...], INNER).astype(BF)
    xt[2 * ROWS : 3 * ROWS] = xa
    xa_copy = to_pair(xt, 2 * ROWS, ROWS)
    qa = nn(xa, wq[...]).astype(BF)
    ka = nn(xa, wk[...]).astype(BF)
    va_t = nn(xa, wv[...]).astype(BF)
    same = (
        (lax.broadcasted_iota(jnp.int32, (2 * ROWS, ROWS), 0) - lax.broadcasted_iota(jnp.int32, (2 * ROWS, ROWS), 1)) & 7
    ) == 0
    gathered(sg, ag, ar1.at[1])
    ga = unfold(ag[...], 256).astype(BF)
    outs = []
    for p in range(5):
        cols = slice(p * 128, (p + 1) * 128)
        o, dq, dk, dv = attend(qa[:, cols], ka[:, cols], va_t[:, cols], ga[:, cols], same)
        outs.append(o)
        dqt[:, cols] = dq.astype(BF)
        dkv[0, 2 * ROWS : 3 * ROWS, cols] = dk.astype(BF)
        dkv[1, 2 * ROWS : 3 * ROWS, cols] = dv.astype(BF)
    so[...] = fold(jnp.concatenate(outs[:3], axis=1), jnp.concatenate(outs[3:], axis=1))
    dn = nt(dqt[...], wq[...]) + nt(dkv[0, 2 * ROWS : 3 * ROWS], wk[...]) + nt(dkv[1, 2 * ROWS : 3 * ROWS], wv[...])
    sd[...] = fold(dn[:, :INNER], dn[:, INNER:])
    scatter(sd, rd, as2.at[0], ar2.at[0])
    scatter(so, ro, as2.at[1], ar2.at[1])
    dt_copy = to_pair(dkv, 2 * ROWS, ROWS, pl.ds(0, INNER))

    xn_copy.wait_recv()
    permute(0, 2 * ROWS)
    xa_copy.wait_recv()
    permute(2 * ROWS, 4 * ROWS)

    cond = vs[0].astype(F32) * (who // 2 == me // 2).astype(F32)
    for d in SLOTS:
        if d:
            video_copies[d].wait_recv()
            cond = cond + vr[d].astype(F32) * (who // 2 == (me // 2 + 8 - d) % 8).astype(F32)
    cn = (cond * lax.rsqrt(jnp.mean(cond * cond, axis=1, keepdims=True) + EPS)).astype(BF)
    xt[4 * ROWS : 4 * ROWS + VT] = cn
    cn_copy = to_pair(xt, 4 * ROWS, VT)
    zeros = jnp.zeros((KEYS - ROWS - VT, INNER), BF)
    kk[ROWS : ROWS + VT] = nn(cn, wk[...]).astype(BF)
    vv[ROWS : ROWS + VT] = nn(cn, wv[...]).astype(BF)
    kk[ROWS + VT :] = zeros
    vv[ROWS + VT :] = zeros
    real = lax.broadcasted_iota(jnp.int32, (2 * ROWS, KEYS), 1) < ROWS + VT
    late = []
    for a, b in CHUNKS:
        for p in range(a, b):
            cols = slice(p * 128, (p + 1) * 128)
            o, dq, dk, dv = attend(q_v[:, cols], kk[:, cols], vv[:, cols], go_v[:, cols], real)
            ov[:, cols] = o
            dqv[:, cols] = dq.astype(BF)
            for i, t in enumerate((dk.astype(BF), dv.astype(BF))):
                dkv[i, :ROWS, cols] = t[:ROWS]
                dkv[i, 4 * ROWS : 4 * ROWS + VT, cols] = t[ROWS : ROWS + VT]
        span = pl.ds(a * 128, (b - a) * 128)
        late.append((to_pair(dkv, 0, ROWS, span), to_pair(dkv, 4 * ROWS, VT, span)))
    cn_copy.wait_recv()
    permute(4 * ROWS, 4 * ROWS + 2 * VT)
    dt_copy.wait_recv()

    xs, ys = [], []
    for n, (a, b) in enumerate(CHUNKS):
        cols = slice(a * 128, b * 128)
        span = pl.ds(a * 128, (b - a) * 128)
        for copy in late[n]:
            copy.wait_recv()
        for d in (2, 1, 3, 0):
            bx = pl.multiple_of(((x + d) % 4) * 160, 32)
            gx[d, :, cols] = nn(xp[0, pl.ds(bx, 160), :], dkv[0, :, cols]).astype(BF)
            if d:
                xs.append(send(gx.at[d, :, span], rx.at[d - 1, :, span], at_x(d)))
            by = pl.multiple_of(((y + d) % 4) * 160, 32)
            gy[d, :, cols] = nn(xp[1, pl.ds(by, 160), :], dkv[1, :, cols]).astype(BF)
            if d:
                ys.append(send(gy.at[d, :, span], ry.at[d - 1, :, span], at_y(d)))

    gathered(so, ro, ar2.at[1])
    hidden = (ov[...] + unfold(ro[...], 256)).astype(BF)
    block_v[...] = (lat_v[...].astype(F32) + nn(hidden, wo[...])).astype(BF)
    block_out = pltpu.make_async_copy(block_v, block_h, load_sem.at[7])
    block_out.start()
    gathered(sd, rd, ar2.at[0])
    dn = nt(dqv[...], wq[...]) + nt(dkv[0, :ROWS], wk[...]) + nt(dkv[1, :ROWS], wv[...]) + unfold(rd[...], INNER)
    norm = normed[...]
    xf = lat_v[...].astype(F32)
    factor = lax.rsqrt(jnp.mean(xf * xf, axis=1, keepdims=True) + EPS)
    back = ogr_v[...].astype(F32) + factor * (dn - norm * jnp.mean(dn * norm, axis=1, keepdims=True))
    back_v[...] = back.astype(BF)
    back_out = pltpu.make_async_copy(back_v, back_h, load_sem.at[8])
    back_out.start()

    def first_sum(at, g, r, copies, cols):
        total = g[0, :, cols].astype(F32)
        for i, copy in enumerate(copies):
            copy.wait_recv()
            total = total + r[ORDER[i] - 1, :, cols].astype(F32)
        m1[at, :, cols] = total

    def second_send(at, position, s2, r2, peer, cols, span):
        pad = jnp.zeros((8, cols.stop - cols.start), F32)
        copies = []
        for d in ORDER:
            rows = pl.multiple_of(((position + d) % 4) * 40, 8)
            s2[d, :, cols] = jnp.concatenate([m1[at, pl.ds(rows, 40), cols], pad], axis=0).astype(BF)
            copies.append(send(s2.at[d, :, span], r2.at[d - 1, :, span], peer(d)))
        return copies

    def second_sum(at, position, r2, copies, cols):
        total = m1[at, pl.ds(pl.multiple_of(position * 40, 8), 40), cols]
        for i, copy in enumerate(copies):
            copy.wait_recv()
            total = total + r2[ORDER[i] - 1, :, cols].astype(F32)[:40]
        return total.astype(BF)

    x2, y2, zs = [], [], []
    for n, (a, b) in enumerate(CHUNKS):
        cols, span = slice(a * 128, b * 128), pl.ds(a * 128, (b - a) * 128)
        first_sum(0, gx, rx, xs[3 * n : 3 * n + 3], cols)
        x2.append(second_send(0, y, s2x, r2x, at_y, cols, span))
        first_sum(1, gy, ry, ys[3 * n : 3 * n + 3], cols)
        y2.append(second_send(1, x, s2y, r2y, at_x, cols, span))

    slot = lax.broadcasted_iota(jnp.int32, (128, 1), 0)
    sz, sk = slot >> 4, slot & 7
    source = jnp.where(sk < 5, ((slot >> 3) & 1) * 40 + sz * 5 + sk, -1)
    place = (source == lax.broadcasted_iota(jnp.int32, (1, 80), 1)).astype(F32).astype(BF)
    for n, (a, b) in enumerate(CHUNKS):
        cols, span = slice(a * 128, b * 128), pl.ds(a * 128, (b - a) * 128)
        tx = second_sum(0, y, r2x, x2[n], cols)
        ty = second_sum(1, x, r2y, y2[n], cols)
        spread = nn(place[:, :40], tx) + nn(place[:, 40:], ty)
        s3[:, :, cols] = spread.astype(BF).reshape(8, 16, cols.stop - cols.start)
        zs.append([send(s3.at[(z + d) % 8, :, span], r3.at[d - 1, :, span], at_z(d)) for d in FAR])
    for n, (a, b) in enumerate(CHUNKS):
        cols = slice(a * 128, b * 128)
        total = s3[z, :, cols].astype(F32)
        for d, copy in zip(FAR, zs[n]):
            copy.wait_recv()
            total = total + r3[d - 1, :, cols].astype(F32)
        grad_v[:, cols] = total[:5]
        grad_v[:, INNER + a * 128 : INNER + b * 128] = total[8:13]

    grad_out = pltpu.make_async_copy(grad_v, grad_o, load_sem.at[9])
    grad_out.start()
    grad_out.wait()
    block_out.wait()
    back_out.wait()
    for copy in started:
        copy.wait_send()


def finish(a, b, c, a_out, b_out, c_out, a_v, b_v, c_v, sem):
    trio = ((a, a_v, a_out), (b, b_v, b_out), (c, c_v, c_out))
    reads = [pltpu.make_async_copy(t[0], t[1], sem.at[0, i]) for i, t in enumerate(trio)]
    writes = [pltpu.make_async_copy(t[1], t[2], sem.at[1, i]) for i, t in enumerate(trio)]
    for copy in reads:
        copy.start()
    for read, write in zip(reads, writes):
        read.wait()
        write.start()
    for copy in writes:
        copy.wait()


def shards(latents, out_grad, video, owner, w_query, w_key, w_value, w_out):
    hbm = pl.BlockSpec(memory_space=pltpu.HBM)
    deep = 4 * ROWS + 2 * VT
    vm = pltpu.VMEM
    dma = pltpu.SemaphoreType.DMA
    half = ((ROWS, INNER), BF)
    scratch = [
        vm((ROWS, D), BF), vm((ROWS, D), BF),
        vm((D, INNER), BF), vm((D, INNER), BF), vm((D, INNER), BF), vm((INNER, D), BF),
        vm((ROWS, D), BF), vm((ROWS, D), BF), vm((5, D), F32),
        vm((ROWS, D), F32), vm((deep, D), BF),
        vm(*half), vm((KEYS, INNER), BF), vm((KEYS, INNER), BF), vm(*half),
        vm((NF, 16, INNER), BF), vm((NF, 16, 384), BF), vm((NF, 16, INNER), BF), vm((NF, 16, 384), BF),
        vm((NF, 16, 384), BF), vm((NF, 16, INNER), BF), vm((NF, 16, 384), BF), vm((NF, 16, INNER), BF),
        vm((8, VT, D), BF), vm((8, VT, D), BF), vm((8, VT, D), BF), vm((8, VT, D), BF),
        vm((ROWS, INNER), F32), vm(*half), vm(*half), vm((2, deep, INNER), BF),
        vm((2, INNER, D), BF), vm((2, INNER, deep), BF),
        vm((4, 160, INNER), BF), vm((4, 160, INNER), BF), vm((3, 160, INNER), BF), vm((3, 160, INNER), BF),
        vm((4, 48, INNER), BF), vm((4, 48, INNER), BF), vm((3, 48, INNER), BF), vm((3, 48, INNER), BF),
        vm((2, 160, INNER), F32), vm((8, 16, INNER), BF), vm((7, 16, INNER), BF),
        dma((10,)), dma((2, NF)), dma((2, NF)), dma((2, NF)), dma((2, NF)), dma((80,)), dma((80,)),
    ]
    block, back, grads = pl.pallas_call(
        kernel,
        out_shape=(
            jax.ShapeDtypeStruct((ROWS, D), BF),
            jax.ShapeDtypeStruct((ROWS, D), BF),
            jax.ShapeDtypeStruct((5, D), F32),
        ),
        in_specs=[hbm, hbm, hbm, pl.BlockSpec(memory_space=pltpu.SMEM)] + [hbm] * 4,
        out_specs=(hbm, hbm, hbm),
        scratch_shapes=scratch,
        compiler_params=pltpu.CompilerParams(
            collective_id=0, has_side_effects=True, vmem_limit_bytes=62 * 1024 * 1024
        ),
    )(
        latents.reshape(ROWS, D),
        out_grad.reshape(ROWS, D),
        video.reshape(8, 2, VT, D),
        owner,
        w_query,
        w_key,
        w_value,
        w_out,
    )
    block, back, grads = pl.pallas_call(
        finish,
        out_shape=(
            jax.ShapeDtypeStruct((ROWS, D), BF),
            jax.ShapeDtypeStruct((ROWS, D), BF),
            jax.ShapeDtypeStruct((5, D), F32),
        ),
        in_specs=[hbm] * 3,
        out_specs=[hbm] * 3,
        scratch_shapes=[vm((ROWS, D), BF), vm((ROWS, D), BF), vm((5, D), F32), dma((2, 3))],
        compiler_params=pltpu.CompilerParams(vmem_limit_bytes=62 * 1024 * 1024),
    )(block, back, grads)
    return block.reshape(latents.shape), back.reshape(latents.shape), grads


def solution(mesh):
    tokens = P("dp", "frame", None, None, None)
    return jax.shard_map(
        shards,
        mesh=mesh,
        in_specs=(tokens, tokens, tokens, P("dp"), P(), P(), P(), P()),
        out_specs=(tokens, tokens, P(("dp", "frame"), None)),
        check_vma=False,
    )
```

time: 76.5 us -> 59.9 us (0.78)
  Pallas kernels: 66.8 us -> 57.7 us
  local copies, waits for them, and re-layouts: 8.18 us -> 0 us
    pallas_call x1, Pallas kernels: 66.8 us -> 55.8 us  [shards(): pl.pallas_call(kernel, out_shape=(jax.ShapeDtypeStruct((ROWS, D), BF), ja...]
    unnamed x13 -> x0, local copies, waits for them, and re-layouts: 8.18 us -> none
    pallas_call x0 -> x1, Pallas kernels: none -> 1.86 us  [shards(): pl.pallas_call(finish, out_shape=(jax.ShapeDtypeStruct((ROWS, D), BF), ja...]
where the time goes in v2:
time: 59.9 us; the launch traced here: 59.1 us
  Pallas kernels  57.7 us (96%)
  between operations  1.45 us (2%)
    pallas_call x1, Pallas kernels, shards(): pl.pallas_call(kernel, out_shape=(jax.ShapeDtypeStruct((ROWS, D), BF), ja...  55.8 us
    pallas_call x1, Pallas kernels, shards(): pl.pallas_call(finish, out_shape=(jax.ShapeDtypeStruct((ROWS, D), BF), ja...  1.86 us

profile of v2, /device:TPU:2, one launch (start us, length us, event | category | flops | bytes accessed | tf_op | source)
XLA Modules:
  0.0 59.1 jit_solution(17205746373881509377)
XLA Ops:
  1.3 55.8 %shard_map.103 = (bf16[128,1280]{1,0:T(8,128)(2,1)}, bf16[128,1280]{1,0:T(8,128)(2,1)}, f32[5,1280]{1,0:T(8,128)}) custom-call(bf16[128,1280]{1,0:T(8,128)(2,1)} %bitcast.6, bf16[128,1280]{1,0:T(8,128)(2,1)} %bitcast.7, bf16[8,2,32,1280]{3,2,1,0:T(8,128)(2,1)} %bitcast.5, s32[1]{0:T(128)S(6)} %copy.11.own, bf16[1280,640]{1,0:T(8,128)(2,1)} %wq_h.1, ...), custom_call_target="tpu_custom_call" | custom-call | tf_op jit(solution)/shard_map/pallas_call | solution.py:389
  57.1 1.9 %shard_map.104 = (bf16[128,1280]{1,0:T(8,128)(2,1)}, bf16[128,1280]{1,0:T(8,128)(2,1)}, f32[5,1280]{1,0:T(8,128)}) custom-call(bf16[128,1280]{1,0:T(8,128)(2,1)} %get-tuple-element.9.a, bf16[128,1280]{1,0:T(8,128)(2,1)} %get-tuple-element.10.b, f32[5,1280]{1,0:T(8,128)} %get-tuple-element.11.c), custom_call_target="tpu_custom_call" | custom-call | tf_op jit(solution)/shard_map/pallas_call | solution.py:412

commit v3 on v2

--- a/solution.py
+++ b/solution.py
@@ -12,9 +12,9 @@
 ROWS, VT, NF = 128, 32, 16
 KEYS = 256
 EPS = 1e-6
-CHUNKS = ((0, 3), (3, 5))
-TURNS = (8, 7, 9, 6, 10, 5, 11, 4, 12, 3, 13, 2, 14, 1, 15)
-SLOTS = (4, 3, 5, 2, 6, 1, 7, 0)
+CHUNKS = ((0, 2), (2, 5))
+TURNS = (12, 4, 13, 5, 10, 2, 14, 6, 11, 3, 15, 7, 8, 9, 1)
+SLOTS = (6, 2, 5, 1, 7, 3, 4, 0)
 ORDER = (2, 1, 3)
 FAR = (4, 3, 5, 2, 6, 1, 7)
 
@@ -70,8 +70,8 @@
 def kernel(
     lat, ogr, vid, own, wq_h, wk_h, wv_h, wo_h,
     block_h, back_h, grad_o,
-    lat_v, ogr_v, wq, wk, wv, wo, block_v, back_v, grad_v,
-    normed, xt, q_v, kk, vv, go_v, sx, sg, ax, ag, so, sd, ro, rd,
+    own_s, lat_v, ogr_v, wq, wk, wv, wo, block_v, back_v, grad_v,
+    normed, xt, q_v, kk, vv, go_v, sx, ax, so, ro,
     va, vb, vs, vr, ov, dqv, dqt, dkv,
     pt, xp, gx, gy, rx, ry, s2x, s2y, r2x, r2y, m1, s3, r3,
     load_sem, as1, ar1, as2, ar2, ms, mr,
@@ -92,25 +92,33 @@
     def at_z(d):
         return (((z + d) % 8) * 2 + x_lo, me)
 
+    def to_f(d):
+        return ((x_hi + d // 8) % 2) * 8 + ((y + (d // 2) % 4) % 4) * 2 + (c + d) % 2
+
+    def from_f(d):
+        return ((x_hi + d // 8) % 2) * 8 + ((y + 4 - (d // 2) % 4) % 4) * 2 + (c + d) % 2
+
     def at_f(d):
-        return (dp, (me + d) % NF)
+        return (dp, to_f(d))
 
     pair = (dp, me + 1 - 2 * c)
 
     loads = [
         pltpu.make_async_copy(src, dst, load_sem.at[i])
         for i, (src, dst) in enumerate(
-            [(lat, lat_v), (ogr, ogr_v), (wo_h, wo), (wq_h, wq), (wk_h, wk), (wv_h, wv), (vid.at[:, c], va)]
+            [(lat, lat_v), (ogr, ogr_v), (wo_h, wo), (wq_h, wq), (wk_h, wk), (wv_h, wv), (vid, va)]
         )
     ]
     loads[0].start()
 
     barrier = pltpu.get_barrier_semaphore()
-    peers = [at_f(d) for d in range(1, NF)] + [at_x(1), at_x(3)] + [at_z(d) for d in range(1, 8)]
+    peers = [at_z(d) for d in FAR] + [at_x(1), at_x(3)] + [at_f(d) for d in TURNS]
     for peer in peers:
         pl.semaphore_signal(barrier, inc=1, device_id=peer, device_id_type=MESH)
     for copy in loads[1:]:
         copy.start()
+    owner_copy = pltpu.make_async_copy(own, own_s, load_sem.at[10])
+    owner_copy.start()
 
     count = [0]
     started = []
@@ -128,12 +136,12 @@
 
     def scatter(src, dst, ss, rs):
         for d in TURNS:
-            send(src.at[(me + d) % NF], dst.at[me], at_f(d), ss.at[d], rs.at[d])
+            send(src.at[to_f(d)], dst.at[me], at_f(d), ss.at[d], rs.at[d])
 
     def gathered(src, dst, rs):
         dst[me] = src[me]
         for d in TURNS:
-            slot = dst.at[(me + NF - d) % NF]
+            slot = dst.at[from_f(d)]
             pltpu.make_async_remote_copy(
                 src_ref=slot, dst_ref=slot, send_sem=rs.at[d], recv_sem=rs.at[d], device_id=pair, device_id_type=MESH
             ).wait_recv()
@@ -149,18 +157,31 @@
     norm = xf * factor
     normed[...] = norm
     xt[:ROWS] = norm.astype(BF)
-    sx[...] = fold(norm[:, :INNER], norm[:, INNER:])
+    sx[:, :, :INNER] = fold(norm[:, :INNER], norm[:, INNER:])
     loads[1].wait()
     loads[2].wait()
     gf = nt(ogr_v[...], wo[...])
-    sg[...] = fold(gf[:, :384], gf[:, 384:])
+    sx[:, :, INNER:] = fold(gf[:, :384], gf[:, 384:])
     go_v[...] = gf.astype(BF)
 
     pl.semaphore_wait(barrier, len(peers))
-    core_copies = [send(vid.at[(me // 2 + d) % 8, 1 - c], vb.at[d], pair) for d in SLOTS]
+    loads[6].wait()
+    core_copy = send(va.at[:, 1 - c], vb, pair)
     scatter(sx, ax, as1.at[0], ar1.at[0])
-    scatter(sg, ag, as1.at[1], ar1.at[1])
     xn_copy = to_pair(xt, 0, ROWS)
+
+    kk[ROWS + VT :] = jnp.zeros((KEYS - ROWS - VT, INNER), BF)
+    vv[ROWS + VT :] = jnp.zeros((KEYS - ROWS - VT, INNER), BF)
+    owner_copy.wait()
+    who = own_s[0]
+    w = (who % 2 == c).astype(F32)
+    video_copies = {}
+    core_copy.wait_recv()
+    for d in SLOTS:
+        to = ((x_hi + d // 4) % 2) * 4 + (y + d) % 4
+        vs[d] = (va[to, c].astype(F32) * w + vb[to].astype(F32) * (1.0 - w)).astype(BF)
+        if d:
+            video_copies[d] = send(vs.at[d], vr.at[d], (dp, to * 2 + c))
 
     for copy in loads[3:6]:
         copy.wait()
@@ -169,17 +190,6 @@
     kk[:ROWS] = nn(xn, wk[...]).astype(BF)
     vv[:ROWS] = nn(xn, wv[...]).astype(BF)
 
-    who = own[0]
-    loads[6].wait()
-    w = (who % 2 == c).astype(F32)
-    video_copies = {}
-    for copy, d in zip(core_copies, SLOTS):
-        copy.wait_recv()
-        to = (me // 2 + d) % 8
-        vs[d] = (va[to].astype(F32) * w + vb[d].astype(F32) * (1.0 - w)).astype(BF)
-        if d:
-            video_copies[d] = send(vs.at[d], vr.at[d], (dp, to * 2 + c))
-
     new = lax.broadcasted_iota(jnp.int32, (INNER, 1), 0)
     u = (new * 52429) >> 18
     k5 = new - 5 * u
@@ -198,8 +208,11 @@
         for i in range(2):
             xp[i, :, first:last] = nt(pt[i], rows).astype(BF)
 
+    xn_copy.wait_recv()
+    permute(0, 2 * ROWS)
+
     gathered(sx, ax, ar1.at[0])
-    xa = unfold(ax[...], INNER).astype(BF)
+    xa = unfold(ax[:, :, :INNER], INNER).astype(BF)
     xt[2 * ROWS : 3 * ROWS] = xa
     xa_copy = to_pair(xt, 2 * ROWS, ROWS)
     qa = nn(xa, wq[...]).astype(BF)
@@ -208,8 +221,7 @@
     same = (
         (lax.broadcasted_iota(jnp.int32, (2 * ROWS, ROWS), 0) - lax.broadcasted_iota(jnp.int32, (2 * ROWS, ROWS), 1)) & 7
     ) == 0
-    gathered(sg, ag, ar1.at[1])
-    ga = unfold(ag[...], 256).astype(BF)
+    ga = unfold(ax[:, :, INNER:], 256).astype(BF)
     outs = []
     for p in range(5):
         cols = slice(p * 128, (p + 1) * 128)
@@ -218,15 +230,12 @@
         dqt[:, cols] = dq.astype(BF)
         dkv[0, 2 * ROWS : 3 * ROWS, cols] = dk.astype(BF)
         dkv[1, 2 * ROWS : 3 * ROWS, cols] = dv.astype(BF)
-    so[...] = fold(jnp.concatenate(outs[:3], axis=1), jnp.concatenate(outs[3:], axis=1))
+    so[:, :, INNER:] = fold(jnp.concatenate(outs[:3], axis=1), jnp.concatenate(outs[3:], axis=1))
     dn = nt(dqt[...], wq[...]) + nt(dkv[0, 2 * ROWS : 3 * ROWS], wk[...]) + nt(dkv[1, 2 * ROWS : 3 * ROWS], wv[...])
-    sd[...] = fold(dn[:, :INNER], dn[:, INNER:])
-    scatter(sd, rd, as2.at[0], ar2.at[0])
-    scatter(so, ro, as2.at[1], ar2.at[1])
+    so[:, :, :INNER] = fold(dn[:, :INNER], dn[:, INNER:])
     dt_copy = to_pair(dkv, 2 * ROWS, ROWS, pl.ds(0, INNER))
 
-    xn_copy.wait_recv()
-    permute(0, 2 * ROWS)
+    scatter(so, ro, as2.at[0], ar2.at[0])
     xa_copy.wait_recv()
     permute(2 * ROWS, 4 * ROWS)
 
@@ -234,37 +243,30 @@
     for d in SLOTS:
         if d:
             video_copies[d].wait_recv()
-            cond = cond + vr[d].astype(F32) * (who // 2 == (me // 2 + 8 - d) % 8).astype(F32)
+            cond = cond + vr[d].astype(F32) * (who // 2 == ((x_hi + d // 4) % 2) * 4 + (y + 8 - d) % 4).astype(F32)
     cn = (cond * lax.rsqrt(jnp.mean(cond * cond, axis=1, keepdims=True) + EPS)).astype(BF)
     xt[4 * ROWS : 4 * ROWS + VT] = cn
     cn_copy = to_pair(xt, 4 * ROWS, VT)
-    zeros = jnp.zeros((KEYS - ROWS - VT, INNER), BF)
-    kk[ROWS : ROWS + VT] = nn(cn, wk[...]).astype(BF)
-    vv[ROWS : ROWS + VT] = nn(cn, wv[...]).astype(BF)
-    kk[ROWS + VT :] = zeros
-    vv[ROWS + VT :] = zeros
     real = lax.broadcasted_iota(jnp.int32, (2 * ROWS, KEYS), 1) < ROWS + VT
-    late = []
-    for a, b in CHUNKS:
-        for p in range(a, b):
-            cols = slice(p * 128, (p + 1) * 128)
-            o, dq, dk, dv = attend(q_v[:, cols], kk[:, cols], vv[:, cols], go_v[:, cols], real)
-            ov[:, cols] = o
-            dqv[:, cols] = dq.astype(BF)
-            for i, t in enumerate((dk.astype(BF), dv.astype(BF))):
-                dkv[i, :ROWS, cols] = t[:ROWS]
-                dkv[i, 4 * ROWS : 4 * ROWS + VT, cols] = t[ROWS : ROWS + VT]
-        span = pl.ds(a * 128, (b - a) * 128)
-        late.append((to_pair(dkv, 0, ROWS, span), to_pair(dkv, 4 * ROWS, VT, span)))
-    cn_copy.wait_recv()
-    permute(4 * ROWS, 4 * ROWS + 2 * VT)
-    dt_copy.wait_recv()
-
     xs, ys = [], []
     for n, (a, b) in enumerate(CHUNKS):
-        cols = slice(a * 128, b * 128)
-        span = pl.ds(a * 128, (b - a) * 128)
-        for copy in late[n]:
+        cols, span = slice(a * 128, b * 128), pl.ds(a * 128, (b - a) * 128)
+        kk[ROWS : ROWS + VT, cols] = nn(cn, wk[:, cols]).astype(BF)
+        vv[ROWS : ROWS + VT, cols] = nn(cn, wv[:, cols]).astype(BF)
+        for p in range(a, b):
+            part = slice(p * 128, (p + 1) * 128)
+            o, dq, dk, dv = attend(q_v[:, part], kk[:, part], vv[:, part], go_v[:, part], real)
+            ov[:, part] = o
+            dqv[:, part] = dq.astype(BF)
+            for i, t in enumerate((dk.astype(BF), dv.astype(BF))):
+                dkv[i, :ROWS, part] = t[:ROWS]
+                dkv[i, 4 * ROWS : 4 * ROWS + VT, part] = t[ROWS : ROWS + VT]
+        late = (to_pair(dkv, 0, ROWS, span), to_pair(dkv, 4 * ROWS, VT, span))
+        if n == 0:
+            cn_copy.wait_recv()
+            permute(4 * ROWS, 4 * ROWS + 2 * VT)
+            dt_copy.wait_recv()
+        for copy in late:
             copy.wait_recv()
         for d in (2, 1, 3, 0):
             bx = pl.multiple_of(((x + d) % 4) * 160, 32)
@@ -276,13 +278,12 @@
             if d:
                 ys.append(send(gy.at[d, :, span], ry.at[d - 1, :, span], at_y(d)))
 
-    gathered(so, ro, ar2.at[1])
-    hidden = (ov[...] + unfold(ro[...], 256)).astype(BF)
+    gathered(so, ro, ar2.at[0])
+    hidden = (ov[...] + unfold(ro[:, :, INNER:], 256)).astype(BF)
     block_v[...] = (lat_v[...].astype(F32) + nn(hidden, wo[...])).astype(BF)
     block_out = pltpu.make_async_copy(block_v, block_h, load_sem.at[7])
     block_out.start()
-    gathered(sd, rd, ar2.at[0])
-    dn = nt(dqv[...], wq[...]) + nt(dkv[0, :ROWS], wk[...]) + nt(dkv[1, :ROWS], wv[...]) + unfold(rd[...], INNER)
+    dn = nt(dqv[...], wq[...]) + nt(dkv[0, :ROWS], wk[...]) + nt(dkv[1, :ROWS], wv[...]) + unfold(ro[:, :, :INNER], INNER)
     norm = normed[...]
     xf = lat_v[...].astype(F32)
     factor = lax.rsqrt(jnp.mean(xf * xf, axis=1, keepdims=True) + EPS)
@@ -321,6 +322,7 @@
         x2.append(second_send(0, y, s2x, r2x, at_y, cols, span))
         first_sum(1, gy, ry, ys[3 * n : 3 * n + 3], cols)
         y2.append(second_send(1, x, s2y, r2y, at_x, cols, span))
+
 
     slot = lax.broadcasted_iota(jnp.int32, (128, 1), 0)
     sz, sk = slot >> 4, slot & 7
@@ -371,20 +373,19 @@
     dma = pltpu.SemaphoreType.DMA
     half = ((ROWS, INNER), BF)
     scratch = [
-        vm((ROWS, D), BF), vm((ROWS, D), BF),
+        pltpu.SMEM((1,), jnp.int32), vm((ROWS, D), BF), vm((ROWS, D), BF),
         vm((D, INNER), BF), vm((D, INNER), BF), vm((D, INNER), BF), vm((INNER, D), BF),
         vm((ROWS, D), BF), vm((ROWS, D), BF), vm((5, D), F32),
         vm((ROWS, D), F32), vm((deep, D), BF),
         vm(*half), vm((KEYS, INNER), BF), vm((KEYS, INNER), BF), vm(*half),
-        vm((NF, 16, INNER), BF), vm((NF, 16, 384), BF), vm((NF, 16, INNER), BF), vm((NF, 16, 384), BF),
-        vm((NF, 16, 384), BF), vm((NF, 16, INNER), BF), vm((NF, 16, 384), BF), vm((NF, 16, INNER), BF),
-        vm((8, VT, D), BF), vm((8, VT, D), BF), vm((8, VT, D), BF), vm((8, VT, D), BF),
+        vm((NF, 16, 1024), BF), vm((NF, 16, 1024), BF), vm((NF, 16, 1024), BF), vm((NF, 16, 1024), BF),
+        vm((8, 2, VT, D), BF), vm((8, VT, D), BF), vm((8, VT, D), BF), vm((8, VT, D), BF),
         vm((ROWS, INNER), F32), vm(*half), vm(*half), vm((2, deep, INNER), BF),
         vm((2, INNER, D), BF), vm((2, INNER, deep), BF),
         vm((4, 160, INNER), BF), vm((4, 160, INNER), BF), vm((3, 160, INNER), BF), vm((3, 160, INNER), BF),
         vm((4, 48, INNER), BF), vm((4, 48, INNER), BF), vm((3, 48, INNER), BF), vm((3, 48, INNER), BF),
         vm((2, 160, INNER), F32), vm((8, 16, INNER), BF), vm((7, 16, INNER), BF),
-        dma((10,)), dma((2, NF)), dma((2, NF)), dma((2, NF)), dma((2, NF)), dma((80,)), dma((80,)),
+        dma((11,)), dma((1, NF)), dma((1, NF)), dma((1, NF)), dma((1, NF)), dma((80,)), dma((80,)),
     ]
     block, back, grads = pl.pallas_call(
         kernel,
@@ -393,7 +394,7 @@
             jax.ShapeDtypeStruct((ROWS, D), BF),
             jax.ShapeDtypeStruct((5, D), F32),
         ),
-        in_specs=[hbm, hbm, hbm, pl.BlockSpec(memory_space=pltpu.SMEM)] + [hbm] * 4,
+        in_specs=[hbm] * 8,
         out_specs=(hbm, hbm, hbm),
         scratch_shapes=scratch,
         compiler_params=pltpu.CompilerParams(

time: 59.9 us -> 60.9 us (1.017); the launches traced: 59.1 us -> 60.8 us
  Pallas kernels: 57.7 us -> 59.4 us
    pallas_call x1, Pallas kernels: 55.8 us -> 57.5 us  [shards(): pl.pallas_call(kernel, out_shape=(jax.ShapeDtypeStruct((ROWS, D), BF), ja...]
where the time goes in v3:
time: 60.9 us; the launch traced here: 60.8 us
  Pallas kernels  59.4 us (98%)
  between operations  1.45 us (2%)
    pallas_call x1, Pallas kernels, shards(): pl.pallas_call(kernel, out_shape=(jax.ShapeDtypeStruct((ROWS, D), BF), ja...  57.5 us
    pallas_call x1, Pallas kernels, shards(): pl.pallas_call(finish, out_shape=(jax.ShapeDtypeStruct((ROWS, D), BF), ja...  1.86 us

profile of v3, /device:TPU:2, one launch (start us, length us, event | category | flops | bytes accessed | tf_op | source)
XLA Modules:
  0.0 60.8 jit_solution(13575828646201322233)
XLA Ops:
  1.3 57.5 %shard_map.103 = (bf16[128,1280]{1,0:T(8,128)(2,1)}, bf16[128,1280]{1,0:T(8,128)(2,1)}, f32[5,1280]{1,0:T(8,128)}) custom-call(bf16[128,1280]{1,0:T(8,128)(2,1)} %bitcast.6, bf16[128,1280]{1,0:T(8,128)(2,1)} %bitcast.7, bf16[8,2,32,1280]{3,2,1,0:T(8,128)(2,1)} %bitcast.5, s32[1]{0:T(128)S(6)} %copy.11.own, bf16[1280,640]{1,0:T(8,128)(2,1)} %wq_h.1, ...), custom_call_target="tpu_custom_call" | custom-call | tf_op jit(solution)/shard_map/pallas_call | solution.py:390
  58.8 1.9 %shard_map.104 = (bf16[128,1280]{1,0:T(8,128)(2,1)}, bf16[128,1280]{1,0:T(8,128)(2,1)}, f32[5,1280]{1,0:T(8,128)}) custom-call(bf16[128,1280]{1,0:T(8,128)(2,1)} %get-tuple-element.9.a, bf16[128,1280]{1,0:T(8,128)(2,1)} %get-tuple-element.10.b, f32[5,1280]{1,0:T(8,128)} %get-tuple-element.11.c), custom_call_target="tpu_custom_call" | custom-call | tf_op jit(solution)/shard_map/pallas_call | solution.py:413

commit v4 on v2

--- a/solution.py
+++ b/solution.py
@@ -13,7 +13,7 @@
 KEYS = 256
 EPS = 1e-6
 CHUNKS = ((0, 3), (3, 5))
-TURNS = (8, 7, 9, 6, 10, 5, 11, 4, 12, 3, 13, 2, 14, 1, 15)
+TURNS = tuple(range(1, 16))
 SLOTS = (4, 3, 5, 2, 6, 1, 7, 0)
 ORDER = (2, 1, 3)
 FAR = (4, 3, 5, 2, 6, 1, 7)

time: 59.9 us -> 59.7 us (level); the launches traced: 59.1 us -> 59.5 us
  no operation moved by 1% of the time
where the time goes in v4:
time: 59.7 us; the launch traced here: 59.5 us
  Pallas kernels  58.1 us (97%)
  between operations  1.45 us (2%)
    pallas_call x1, Pallas kernels, shards(): pl.pallas_call(kernel, out_shape=(jax.ShapeDtypeStruct((ROWS, D), BF), ja...  56.2 us
    pallas_call x1, Pallas kernels, shards(): pl.pallas_call(finish, out_shape=(jax.ShapeDtypeStruct((ROWS, D), BF), ja...  1.86 us

profile of v4, /device:TPU:2, one launch (start us, length us, event | category | flops | bytes accessed | tf_op | source)
XLA Modules:
  0.0 59.5 jit_solution(13561325390988861193)
XLA Ops:
  1.3 56.2 %shard_map.103 = (bf16[128,1280]{1,0:T(8,128)(2,1)}, bf16[128,1280]{1,0:T(8,128)(2,1)}, f32[5,1280]{1,0:T(8,128)}) custom-call(bf16[128,1280]{1,0:T(8,128)(2,1)} %bitcast.6, bf16[128,1280]{1,0:T(8,128)(2,1)} %bitcast.7, bf16[8,2,32,1280]{3,2,1,0:T(8,128)(2,1)} %bitcast.5, s32[1]{0:T(128)S(6)} %copy.11.own, bf16[1280,640]{1,0:T(8,128)(2,1)} %wq_h.1, ...), custom_call_target="tpu_custom_call" | custom-call | tf_op jit(solution)/shard_map/pallas_call | solution.py:389
  57.5 1.9 %shard_map.104 = (bf16[128,1280]{1,0:T(8,128)(2,1)}, bf16[128,1280]{1,0:T(8,128)(2,1)}, f32[5,1280]{1,0:T(8,128)}) custom-call(bf16[128,1280]{1,0:T(8,128)(2,1)} %get-tuple-element.9.a, bf16[128,1280]{1,0:T(8,128)(2,1)} %get-tuple-element.10.b, f32[5,1280]{1,0:T(8,128)} %get-tuple-element.11.c), custom_call_target="tpu_custom_call" | custom-call | tf_op jit(solution)/shard_map/pallas_call | solution.py:412
